TPU v7x, 512 devices: a whole 4x4x16 slice. The times are simulated.
512 devices in a mesh: section: 4 (over x_lo, core), tm: 8 (over y, x_hi), space: 16 (over z).
Axes of the slice: x: 4 (x_hi: 2, x_lo: 2; x = x_hi * 2 + x_lo), y: 4, z: 16, core: 2. Of those that a mesh axis runs over, the one named last changes fastest.
Arguments:
- hidden_in: bfloat16 [4, 8, 2048, 1152], P('section', 'tm', 'space'), may hold values from -6 to 6
- query_s: bfloat16 [4, 8, 2048, 1152], P('section', 'tm', 'space'), may hold values from -8 to 8
- key_s: bfloat16 [4, 8, 2048, 1152], P('section', 'tm', 'space'), may hold values from -8 to 8
- value_s: bfloat16 [4, 8, 2048, 1152], P('section', 'tm', 'space'), may hold values from -6 to 6
- out_proj_s: bfloat16 [4, 1152, 1152], P('section', 'space'), may hold values from -0.1875 to 0.1875
- gate_s: float32 [4, 1152], P('section'), may hold values from 0.1 to 1.9
- shift_t: float32 [4, 1152], P('section'), may hold values from -3 to 3
- scale_t: float32 [4, 1152], P('section'), may hold values from -3 to 3
- qkv_t: bfloat16 [4, 3, 1152, 1152], P('section', None, 'tm'), may hold values from -0.1875 to 0.1875
- out_t: bfloat16 [4, 1152, 1152], P('section', 'tm'), may hold values from -0.1875 to 0.1875
- gate_t: float32 [4, 1152], P('section'), may hold values from 0.1 to 1.9
Outputs:
- handed: bfloat16 [4, 8, 2048, 1152], P('section', 'tm', 'space')
All inputs are finite; a program needn't handle non-finite values.
Results may differ from a plain program's by a relative error of at most 0.022.
Values may be sent and summed in bfloat16 or wider, within the bound.
A program may use at most 64 MiB of HBM per device.

v0:
```python
import jax
import jax.numpy as jnp
from jax import lax
from jax.sharding import PartitionSpec as P

HEADS = 16


def passed_along(block, axis, distance):
    devices = range(lax.axis_size(axis))
    route = [((i - distance) % len(devices), i) for i in devices]
    return lax.ppermute(block, axis, route)


def absorb_keys(carry, queries_split, keys_block, values_block, factor):
    running_max, denominator, weighted = carry
    scores = (
        jnp.einsum("fqhd,fkhd->fhqk", queries_split, keys_block, preferred_element_type=jnp.float32)
        * factor
    )
    newest_max = jnp.maximum(running_max, jnp.max(scores, axis=-1))
    shrink_factor = jnp.exp(running_max - newest_max)
    exponents = jnp.exp(scores - newest_max[..., None])
    denominator = denominator * shrink_factor + jnp.sum(exponents, axis=-1)
    weighted = weighted * shrink_factor[..., None] + jnp.einsum(
        "fhqk,fkhd->fhqd",
        exponents.astype(jnp.bfloat16),
        values_block,
        preferred_element_type=jnp.float32,
    )
    return (newest_max, denominator, weighted)


def keyed_attention(queries, keys_local, values_local):
    frames, patches, width = queries.shape
    head_dim = width // HEADS
    factor = head_dim ** (-0.5)
    queries_split = queries.reshape(frames, patches, HEADS, head_dim)
    initial = (
        jnp.full((frames, HEADS, patches), -jnp.inf, jnp.float32),
        jnp.zeros((frames, HEADS, patches), jnp.float32),
        jnp.zeros((frames, HEADS, patches, head_dim), jnp.float32),
    )
    key_rows = lax.all_gather(keys_local, "space", axis=1, tiled=True).reshape(
        frames, -1, HEADS, head_dim
    )
    value_rows = lax.all_gather(values_local, "space", axis=1, tiled=True).reshape(
        frames, -1, HEADS, head_dim
    )
    count = key_rows.shape[1]
    blocks = count // 512
    key_blocks = jnp.moveaxis(key_rows.reshape(frames, blocks, 512, HEADS, head_dim), 1, 0)
    value_blocks = jnp.moveaxis(value_rows.reshape(frames, blocks, 512, HEADS, head_dim), 1, 0)

    def step_block(inner, pair):
        return (absorb_keys(inner, queries_split, pair[0], pair[1], factor), None)

    final_max, denominator, weighted = lax.scan(step_block, initial, (key_blocks, value_blocks))[0]
    attended = (weighted / denominator[..., None]).astype(jnp.bfloat16)
    return jnp.transpose(attended, (0, 2, 1, 3)).reshape(frames, patches, width)


def shards(
    hidden_in, query_s, key_s, value_s, out_proj_s, gate_s, shift_t, scale_t, qkv_t, out_t, gate_t
):
    queries = query_s[0]
    frames, patches, width = queries.shape
    head_dim = width // HEADS
    attended = keyed_attention(queries, key_s[0], value_s[0])
    flat_attended = attended.reshape(frames * patches, width)
    projected = jnp.dot(
        flat_attended,
        lax.all_gather(out_proj_s[0], "space", axis=0, tiled=True),
        preferred_element_type=jnp.float32,
    )
    middle = (
        hidden_in[0].reshape(frames * patches, width).astype(jnp.float32) + gate_s[0] * projected
    ).astype(jnp.bfloat16)
    widened = middle.astype(jnp.float32)
    mean_value = jnp.mean(widened, axis=-1, keepdims=True)
    centred = widened - mean_value
    variance = jnp.mean(centred * centred, axis=-1, keepdims=True)
    normed = (centred * lax.rsqrt(variance + 1e-06) * (1.0 + scale_t[0]) + shift_t[0]).astype(
        jnp.bfloat16
    )
    weights_qkv = qkv_t[0]
    projections = jnp.einsum(
        "fpd,ced->cefp",
        lax.all_gather(normed.reshape(frames, patches, width), "tm", axis=0, tiled=True),
        weights_qkv,
        preferred_element_type=jnp.float32,
    ).astype(jnp.bfloat16)
    local_features = projections.shape[1]
    all_frames = projections.shape[2]
    split_proj = projections.reshape(3, local_features // head_dim, head_dim, all_frames, patches)
    scores = jnp.einsum(
        "hdfp,hdgp->hfgp", split_proj[0], split_proj[1], preferred_element_type=jnp.float32
    ) * head_dim ** (-0.5)
    weights = jax.nn.softmax(scores, axis=2).astype(jnp.bfloat16)
    mixed = jnp.einsum(
        "hfgp,hdgp->hdfp", weights, split_proj[2], preferred_element_type=jnp.float32
    ).astype(jnp.bfloat16)
    mixed_local = mixed.reshape(local_features, all_frames, patches)
    returned = lax.all_to_all(mixed_local, "tm", split_axis=1, concat_axis=0, tiled=True)
    mixed_all = returned.reshape(width, frames * patches)
    summed = jnp.einsum(
        "et,ed->td",
        mixed_all,
        lax.all_gather(out_t[0], "tm", axis=0, tiled=True),
        preferred_element_type=jnp.float32,
    )
    finished = (middle.astype(jnp.float32) + gate_t[0] * summed).astype(jnp.bfloat16)
    return passed_along(finished.reshape(1, frames, patches, width), "section", 1)


def solution(mesh):
    in_specs = (
        P("section", "tm", "space", None),
        P("section", "tm", "space", None),
        P("section", "tm", "space", None),
        P("section", "tm", "space", None),
        P("section", "space", None),
        P("section", None),
        P("section", None),
        P("section", None),
        P("section", None, "tm", None),
        P("section", "tm", None),
        P("section", None),
    )
    out_specs = P("section", "tm", "space", None)
    return jax.shard_map(shards, mesh=mesh, in_specs=in_specs, out_specs=out_specs, check_vma=False)
```

profile of v0, /device:TPU:1, one launch (start us, length us, event | category | flops | bytes accessed | tf_op | source)
XLA Modules:
  0.0 408.4 jit_solution(6367944884733432690)
XLA Ops:
  6.5 0.7 all-gather.11.cloned.1.call-update
  7.3 0.7 all-gather.13.cloned.1.call-update
  8.1 0.7 all-gather.15.cloned.1.call-update
  8.8 1.2 copy.44
  10.0 0.7 add_reduce_fusion
  10.7 0.7 reduce.4
  11.4 0.7 reduce.7
  12.1 74.8 %all-gather.11.cloned.1.call-done = bf16[1,1,2048,1152]{3,2,1,0:T(8,128)(2,1)} async-done(((bf16[1,1,128,1152]{3,2,1,0:T(8,128)(2,1)}), bf16[1,1,2048,1152]{3,2,1,0:T(8,128)(2,1)}) %all-gather.11.cloned.1.call-update) | async-done | bytes 4718608 | tf_op jit(solution)/shard_map/all_gather | solution.py:44
  86.9 17.4 %reshape.83 = bf16[4,1,512,16,72]{4,3,2,0,1:T(8,128)(2,1)} reshape(bf16[1,1,2048,1152]{3,2,1,0:T(8,128)(2,1)} %all-gather.11.cloned.1.call-done) | data formatting | bytes 9437184 | tf_op jit(solution)/shard_map/transpose;reshape;reshape | solution.py:52
  104.3 13.2 %copy.46 = bf16[4,1,512,16,72]{2,4,3,1,0:T(8,128)(2,1)} copy(bf16[4,1,512,16,72]{4,3,2,0,1:T(8,128)(2,1)} %reshape.83) | data formatting | bytes 9437184
  117.5 47.3 %all-gather.13.cloned.1.call-done = bf16[1,1,2048,1152]{3,2,1,0:T(8,128)(2,1)} async-done(((bf16[1,1,128,1152]{3,2,1,0:T(8,128)(2,1)}), bf16[1,1,2048,1152]{3,2,1,0:T(8,128)(2,1)}) %all-gather.13.cloned.1.call-update) | async-done | bytes 4718608 | tf_op jit(solution)/shard_map/all_gather | solution.py:47
  164.8 17.4 %reshape.84 = bf16[4,1,512,16,72]{4,3,2,0,1:T(8,128)(2,1)} reshape(bf16[1,1,2048,1152]{3,2,1,0:T(8,128)(2,1)} %all-gather.13.cloned.1.call-done) | data formatting | bytes 9437184 | tf_op jit(solution)/shard_map/transpose;reshape;reshape | solution.py:53
  182.2 13.1 %copy.47 = bf16[4,1,512,16,72]{2,4,3,1,0:T(8,128)(2,1)} copy(bf16[4,1,512,16,72]{4,3,2,0,1:T(8,128)(2,1)} %reshape.84) | data formatting | bytes 9437184
  195.4 34.6 %while.15 = (s32[]{:T(128)}, f32[1,16,128]{2,1,0:T(8,128)S(1)}, f32[1,16,128]{2,1,0:T(8,128)S(1)}, f32[1,16,128,72]{2,3,1,0:T(8,128)S(1)}, bf16[4,1,512,16,72]{2...) while((s32[]{:T(128)}, f32[1,16,128]{2,1,0:T(8,128)S(1)}, ...), condition=%wide.region_3.4_spmd.clone, body=%wide.region_0.3_spmd.clone.sunk | while | flops 310833152 | bytes 33326212 | solution.py:58
  195.4 4.1 %bitcast_reduce_fusion.3 = (f32[16,128]{1,0:T(8,128)S(1)}, f32[16,512,128]{2,1,0:T(8,128)}) fusion(bf16[1,128,16,72]{1,3,2,0:T(8,128)(2,1)S(1)} %get-tuple-element.189, bf16[4,1,512,16,72]{2,4,3,1,0:T(8,128)(2,1)} %get-tuple-element.188, s32[]{:T(128)} %get-tuple-element.175), kind=kOutput, calls=%fused_computation.1.clone.1 | convolution fusion | flops 153090048 | bytes 5677568 | tf_op jit(solution)/shard_map/while/body/eval_jaxpr/fqhd,fkhd->fhqk/dot_general | solution.py:18
  199.5 3.7 fusion.81
  203.3 0.7 fusion.80
  204.1 4.0 bitcast_reduce_fusion.3
  208.1 3.7 fusion.81
  212.0 0.7 fusion.80
  212.7 4.1 bitcast_reduce_fusion.3
  216.8 3.7 fusion.81
  220.6 0.7 fusion.80
  221.4 4.0 bitcast_reduce_fusion.3
  225.4 3.7 fusion.81
  229.3 0.7 fusion.80
  230.1 6.4 %all-gather.15.cloned.1.call-done = bf16[1,1152,1152]{2,1,0:T(8,128)(2,1)} async-done(((bf16[1,72,1152]{2,1,0:T(8,128)(2,1)}), bf16[1,1152,1152]{2,1,0:T(8,128)(2,1)}) %all-gather.15.cloned.1.call-update) | async-done | bytes 2654224 | tf_op jit(solution)/shard_map/all_gather | solution.py:73
  236.5 2.5 fusion.62
  239.0 0.2 multiply_reduce_fusion
  239.2 0.9 add_convert_fusion
  240.2 0.5 all-gather.19.cloned.1.call-update
  240.7 76.2 %all-gather.17.cloned.1.call-done = bf16[1024,1152]{1,0:T(8,128)(2,1)} async-done(((bf16[128,1152]{1,0:T(8,128)(2,1)}), bf16[1024,1152]{1,0:T(8,128)(2,1)}) %all-gather.17.cloned.1.call-update) | async-done | bytes 2359312 | tf_op jit(solution)/shard_map/all_gather | solution.py:89
  316.9 3.0 fusion.52
  319.9 0.3 copy.48
  320.3 1.1 copy.49
  321.4 1.5 fusion.64
  322.8 0.3 copy.50
  323.1 0.6 fusion.63
  323.7 0.3 copy.52
  324.1 0.3 copy.51
  324.4 0.4 fusion.53
  324.8 1.0 copy.61
  325.8 3.4 all-to-all-start
  329.3 62.6 %all-gather.19.cloned.1.call-done = bf16[1,1152,1152]{2,1,0:T(8,128)(2,1)} async-done(((bf16[1,144,1152]{2,1,0:T(8,128)(2,1)}), bf16[1,1152,1152]{2,1,0:T(8,128)(2,1)}) %all-gather.19.cloned.1.call-update) | async-done | bytes 2654224 | tf_op jit(solution)/shard_map/all_gather | solution.py:109
  391.9 2.4 fusion.49
  394.3 3.2 collective-permute-start
  397.5 3.6 collective-permute-done
  401.1 0.7 copy.75
  (42 shorter events, 1.0 us)
Async XLA Ops:
  6.5 310.3 %copy-start = (bf16[1,3,144,1152]{3,2,1,0:T(8,128)(2,1)S(1)}, bf16[1,3,144,1152]{3,2,1,0:T(8,128)(2,1)}, u32[]{:S(2)}) copy-start(bf16[1,3,144,1152]{3,2,1,0:T(8,128)(2,1)} %param.21) | copy-start | bytes 2985988
  6.5 80.4 %all-gather.11.cloned.1.call-start = ((), (), s32[]{:S(2)}) async-start(), calls=%async_computation.1 | async-start | bytes 5013504 | tf_op jit(solution)/shard_map/all_gather | solution.py:44
  7.3 157.5 %all-gather.13.cloned.1.call-start = ((), (), s32[]{:S(2)}) async-start(), calls=%async_computation.2 | async-start | bytes 5013504 | tf_op jit(solution)/shard_map/all_gather | solution.py:47
  8.0 228.5 %all-gather.15.cloned.1.call-start = ((), (), s32[]{:S(2)}) async-start(), calls=%async_computation.3 | async-start | bytes 2820096 | tf_op jit(solution)/shard_map/all_gather | solution.py:73
  8.7 308.1 %all-gather.17.cloned.1.call-start = ((), (), s32[]{:S(2)}) async-start(), calls=%async_computation.4 | async-start | bytes 2654208 | tf_op jit(solution)/shard_map/all_gather | solution.py:89
  195.4 41.1 %copy-start.2 = (bf16[1,1,128,1152]{3,2,1,0:T(8,128)(2,1)S(1)}, bf16[1,1,128,1152]{3,2,1,0:T(8,128)(2,1)}, u32[]{:S(2)}) copy-start(bf16[1,1,128,1152]{3,2,1,0:T(8,128)(2,1)} %param.13) | copy-start | bytes 884740
  199.5 3.9 copy-start.1
  208.1 3.9 copy-start.1
  216.8 3.9 copy-start.1
  225.4 3.9 copy-start.1
  240.1 151.8 %all-gather.19.cloned.1.call-start = ((), (), s32[]{:S(2)}) async-start(), calls=%async_computation.5 | async-start | bytes 2985984 | tf_op jit(solution)/shard_map/all_gather | solution.py:109
  320.3 9.0 %copy-start.3 = (f32[1,1152]{1,0:T(1,128)S(1)}, f32[1,1152]{1,0:T(1,128)}, u32[]{:S(2)}) copy-start(f32[1,1152]{1,0:T(1,128)} %param.23) | copy-start | bytes 13828
  325.8 66.1 %all-to-all-start = ((bf16[144,8,128]{2,0,1:T(8,128)(2,1)}), bf16[144,8,128]{2,0,1:T(8,128)(2,1)S(1)}, u32[]{:S(2)}, u32[]{:S(2)}) async-start(bf16[144,8,128]{2,0,1:T(8,128)(2,1)} %bitcast.18), calls=%async_computation | async-start | bytes 589824 | tf_op jit(solution)/shard_map/all_to_all | solution.py:104
  394.3 6.8 %collective-permute-start = (bf16[1,1,128,1152]{3,2,1,0:T(8,128)(2,1)S(1)}, bf16[1,1,128,1152]{3,2,1,0:T(8,128)(2,1)S(1)}, u32[]{:S(2)}, u32[]{:S(2)}) collective-permute-start(bf16[1,1,128,1152]{3,2,1,0:T(8,128)(2,1)S(1)} %fusion.49), channel_id=1, source_target_pairs={{384,0},{0,128},{128,256},{256,384},{385,1},{1,129},{129,257},{257... | collective-permute-start | bytes 884744 | tf_op jit(solution)/shard_map/ppermute | solution.py:12
Sparse Core Ops, SparseCore 0:
  9.4 77.4 all-gather.10
  89.0 75.7 all-gather.12
  166.9 69.5 all-gather.14
  240.2 76.5 all-gather.16
  319.9 71.9 all-gather.18
where the time goes:
time: 410 us; the launch traced here: 408 us
  waiting for transfers between devices  274 us (67%)
  local copies, waits for them, and re-layouts  67 us (16%)
  matrix products  40.8 us (10%)
  between operations  13.3 us (3%)
  other arithmetic  6.79 us (2%)
  starting transfers between devices  6.74 us (2%)
    all_gather x1, waiting for transfers between devices, shards(): lax.all_gather(normed.reshape(frames, patches, width), 'tm', axis=0, tile...  76.2 us
    all_gather x1, waiting for transfers between devices, keyed_attention(): lax.all_gather(keys_local, 'space', axis=1, tiled=True)  74.8 us
    all_gather x1, waiting for transfers between devices, shards(): lax.all_gather(out_t[0], 'tm', axis=0, tiled=True)  62.6 us
    all_gather x1, waiting for transfers between devices, keyed_attention(): lax.all_gather(values_local, 'space', axis=1, tiled=True)  47.3 us
    unnamed x10, local copies, waits for them, and re-layouts  28.2 us
    another operation x1, local copies, waits for them, and re-layouts, keyed_attention(): jnp.moveaxis(key_rows.reshape(frames, blocks, 512, HEADS, head_dim), 1, 0)  17.4 us
    another operation x1, local copies, waits for them, and re-layouts, keyed_attention(): jnp.moveaxis(value_rows.reshape(frames, blocks, 512, HEADS, head_dim), 1, 0)  17.4 us
    dot_general x4, matrix products, absorb_keys(): jnp.einsum('fqhd,fkhd->fhqk', queries_split, keys_block, preferred_elemen...  16.2 us
  transfers between devices with their start and end apart: 7, of which 6 were waited for; matrix products, arithmetic and copies ran while one was open for 26% of the time, Pallas kernels for 0%

commit v1 on v0

v1 whole, which is shorter than its diff:
```python
import jax
import jax.numpy as jnp
from jax import lax
from jax.experimental import pallas as pl
from jax.experimental.pallas import tpu as pltpu
from jax.sharding import PartitionSpec as P

MESH = pl.DeviceIdType.MESH
F32 = jnp.float32
BF16 = jnp.bfloat16
D = 1152
HD = 72
NZ = 16
NT = 8
NS = 4
ROWS = 128
PART = 32
FACTOR = HD ** (-0.5)


def kernel(
    q_ref, k_ref, v_ref, hid_hbm, w_ref, gs_ref, sh_ref, sc_ref, qkv_hbm, ot_hbm, gt_ref,
    out_ref,
    kvs, kvr, qs, qr, osd, orc, wz, wt, wfull, kmat, vmat, ofull, wq, wo, hid, mids, midr, mixt, fins, finr,
    skv, rkv, sq, rq, so, ro, sw, rw, swy, rwy, swx, rwx, sqy, rqy, sm, rm, sf, rf, loc,
):
    sec = lax.axis_index("section")
    t = lax.axis_index("tm")
    z = lax.axis_index("space")
    y = t // 2
    xh = t % 2
    nxt = (sec + 1) % NS
    prv = (sec + NS - 1) % NS
    zr = {"space": (z + 1) % NZ}
    zl = {"space": (z + NZ - 1) % NZ}
    yr = {"tm": (t + 2) % NT}
    yl = {"tm": (t + NT - 2) % NT}
    xo = {"tm": t + 1 - 2 * xh}
    t_yr = (t + 2) % NT
    t_yl = (t + NT - 2) % NT
    t_y2 = (t + 4) % NT
    y_r = (y + 1) % 4
    y_l = (y + 3) % 4
    y_2 = (y + 2) % 4

    def remote(src, dst, s_sem, r_sem, dev):
        return pltpu.make_async_remote_copy(
            src_ref=src, dst_ref=dst, send_sem=s_sem, recv_sem=r_sem, device_id=dev, device_id_type=MESH
        )

    barrier = pltpu.get_barrier_semaphore()

    def greet_z(i, c):
        pl.semaphore_signal(barrier, inc=1, device_id={"space": (z + i) % NZ}, device_id_type=MESH)
        return c

    lax.fori_loop(1, NZ, greet_z, 0)

    def greet_t(i, c):
        pl.semaphore_signal(barrier, inc=1, device_id={"tm": (t + i) % NT}, device_id_type=MESH)
        return c

    lax.fori_loop(1, NT, greet_t, 0)

    def greet_s(i, c):
        pl.semaphore_signal(barrier, inc=1, device_id={"section": nxt, "tm": i}, device_id_type=MESH)
        pl.semaphore_signal(barrier, inc=1, device_id={"section": prv, "tm": i}, device_id_type=MESH)
        return c

    lax.fori_loop(0, NT, greet_s, 0)

    loc_q = pltpu.make_async_copy(qkv_hbm, wq.at[y], loc.at[0])
    loc_o = pltpu.make_async_copy(ot_hbm, wo.at[y], loc.at[1])
    loc_h = pltpu.make_async_copy(hid_hbm, hid, loc.at[2])
    loc_q.start()
    loc_o.start()
    loc_h.start()

    wz[z, 0] = w_ref[:, pl.ds(pl.multiple_of(t * 128, 128), 128)]
    wz[z, 1] = w_ref[:, 1024:1152]
    kt = k_ref[...].astype(F32).T
    vt = v_ref[...].astype(F32).T
    for h in range(NZ):
        kvs[h] = jnp.concatenate([kt[HD * h : HD * (h + 1)], vt[HD * h : HD * (h + 1)]], axis=0).astype(BF16)
    qt = q_ref[...].astype(F32).T
    for h in range(NZ):
        qs[h] = qt[HD * h : HD * (h + 1)].astype(BF16)
    kvr[z] = kvs[z]
    qr[z] = qs[z]

    pl.semaphore_wait(barrier, (NZ - 1) + (NT - 1) + 2 * NT)

    def ring_right(j):
        src = (z + NZ - j) % NZ
        return remote(wz.at[src], wz.at[src], sw.at[0, j], rw.at[0, j], zr)

    def ring_left(j):
        src = (z + j) % NZ
        return remote(wz.at[src], wz.at[src], sw.at[1, j], rw.at[1, j], zl)

    def ring_right_half():
        src = (z + NZ - 7) % NZ
        return remote(wz.at[src, 0], wz.at[src, 0], sw.at[0, 7], rw.at[0, 7], zr)

    def ring_left_half():
        src = (z + 7) % NZ
        return remote(wz.at[src, 1], wz.at[src, 1], sw.at[1, 7], rw.at[1, 7], zl)

    ring_right(0).start()
    ring_left(0).start()

    def wq_send(unit, way):
        dev = yr if way == 0 else yl
        if unit < 3:
            return remote(qkv_hbm.at[unit], wq.at[y, unit], sqy.at[way, unit], rqy.at[way, unit], dev)
        return remote(ot_hbm, wo.at[y], sqy.at[way, 3], rqy.at[way, 3], dev)

    for unit in (0, 1, 2, 3):
        wq_send(unit, 0).start()
        wq_send((unit + 2) % 4, 1).start()

    def kv_copy(i):
        to = (z + i) % NZ
        return remote(kvs.at[to], kvr.at[z], skv.at[i], rkv.at[i], {"space": to})

    def q_copy(i):
        to = (z + i) % NZ
        return remote(qs.at[to], qr.at[z], sq.at[i], rq.at[i], {"space": to})

    def kv_start(i, c):
        kv_copy(NZ - i).start()
        kv_copy(i).start()
        return c

    lax.fori_loop(1, 8, kv_start, 0)
    kv_copy(8).start()

    def q_start(i, c):
        q_copy(i).start()
        q_copy(NZ - i).start()
        return c

    lax.fori_loop(1, 8, q_start, 0)
    q_copy(8).start()

    def ring_step(j, c):
        ring_right(j - 1).wait_recv()
        ring_right(j).start()
        ring_left(j - 1).wait_recv()
        ring_left(j).start()
        return c

    lax.fori_loop(1, 7, ring_step, 0)
    ring_right(6).wait_recv()
    ring_right_half().start()
    ring_left(6).wait_recv()
    ring_left_half().start()
    ring_right_half().wait_recv()
    ring_left_half().wait_recv()

    wt[t] = wz[:, 0]

    def wy_copy(way):
        return remote(wt.at[t], wt.at[t], swy.at[way], rwy.at[way], yr if way == 0 else yl)

    def wx_copy(i, tt):
        return remote(wt.at[tt], wt.at[tt], swx.at[i], rwx.at[i], xo)

    wy_copy(0).start()
    wy_copy(1).start()
    wx_copy(0, t).start()

    def take_kv(src):
        block = kvr[src].astype(F32)
        off = pl.ds(pl.multiple_of(src * ROWS, ROWS), ROWS)
        kmat[off, :] = block[:HD].T.astype(BF16)
        vmat[:HD, off] = block[HD:].astype(BF16)

    vmat[HD:, :] = jnp.ones((8, NZ * ROWS), BF16)
    take_kv(z)

    def kv_take(i, c):
        kv_copy(i).wait_recv()
        take_kv((z + NZ - i) % NZ)
        return c

    lax.fori_loop(1, NZ, kv_take, 0)

    def wq_pass(unit, way):
        dev, yy = (yr, y_l) if way == 0 else (yl, y_r)
        if unit < 3:
            return remote(wq.at[yy, unit], wq.at[yy, unit], sqy.at[way, 4 + unit], rqy.at[way, 4 + unit], dev)
        return remote(wo.at[yy], wo.at[yy], sqy.at[way, 7], rqy.at[way, 7], dev)

    def wy_pass(way):
        dev, tt = (yr, t_yl) if way == 0 else (yl, t_yr)
        part = wt.at[tt, pl.ds(8 * way, 8)]
        return remote(part, part, swy.at[2 + way], rwy.at[2 + way], dev)

    wy_copy(0).wait_recv()
    wy_pass(0).start()
    wx_copy(1, t_yl).start()
    wy_copy(1).wait_recv()
    wy_pass(1).start()
    wx_copy(2, t_yr).start()
    for unit, way in ((0, 0), (2, 1), (1, 0), (3, 1)):
        wq_send(unit, way).wait_recv()
        wq_pass(unit, way).start()

    def o_copy(i):
        to = (z + i) % NZ
        return remote(osd.at[to], orc.at[z], so.at[i], ro.at[i], {"space": to})

    def attend(d, c):
        src_a = (z + NZ - d) % NZ
        src_b = jnp.where(d == 8, z, (z + d) % NZ)
        q_copy(d).wait_recv()

        @pl.when(d < 8)
        def _():
            q_copy(NZ - d).wait_recv()

        queries = jnp.concatenate([qr[src_a], qr[src_b]], axis=1)
        s = jnp.dot(kmat[...], queries, preferred_element_type=F32)
        top = jnp.max(s, axis=0, keepdims=True)
        p = jnp.exp((s - top) * FACTOR).astype(BF16)
        o = jnp.dot(vmat[...], p, preferred_element_type=F32)
        o = (o[:HD] / o[HD : HD + 1]).astype(BF16)
        osd[src_a] = o[:, :ROWS]
        osd[src_b] = o[:, ROWS:]
        o_copy(NZ - d).start()

        @pl.when(d < 8)
        def _():
            o_copy(d).start()

        @pl.when(d == 4)
        def _():
            wy_pass(0).wait_recv()
            wy_pass(1).wait_recv()
            wx_copy(3, t_y2).start()

        return c

    lax.fori_loop(1, 9, attend, 0)
    orc[z] = osd[z]

    for i, tt in ((0, t), (1, t_yl), (2, t_yr), (3, t_y2)):
        wx_copy(i, tt).wait_recv()

    def w_rows(j, c):
        row = pl.ds(pl.multiple_of(144 * j, 144), 144)
        for b in range(9):
            if b < 8:
                lo, hi = wt[b, 2 * j], wt[b, 2 * j + 1]
            else:
                lo, hi = wz[2 * j, 1], wz[2 * j + 1, 1]
            wfull[row, 128 * b : 128 * (b + 1)] = jnp.concatenate([lo.astype(F32), hi.astype(F32)], axis=0).astype(BF16)
        return c

    lax.fori_loop(0, 8, w_rows, 0)
    loc_h.wait()

    def o_take(i, c):
        o_copy(i).wait_recv()
        src = (z + NZ - i) % NZ
        ofull[pl.ds(pl.multiple_of(src * HD, 8), HD), :] = orc[src].astype(F32)
        return c

    ofull[pl.ds(pl.multiple_of(z * HD, 8), HD), :] = orc[z].astype(F32)
    lax.fori_loop(1, NZ, o_take, 0)
    attended = ofull[...].T.astype(BF16)
    projected = jnp.dot(attended, wfull[...], preferred_element_type=F32)
    mids[...] = (hid[...].astype(F32) + gs_ref[...] * projected).astype(BF16)

    def mid_copy(i):
        to = (t + i) % NT
        rows = pl.ds(pl.multiple_of((to // 2) * PART, PART), PART)
        return remote(mids.at[rows], midr.at[t], sm.at[i], rm.at[i], {"tm": to})

    def mid_start(i, c):
        mid_copy(i).start()
        return c

    lax.fori_loop(1, NT, mid_start, 0)
    midr[t] = mids[pl.ds(pl.multiple_of(y * PART, PART), PART), :]

    loc_q.wait()
    loc_o.wait()
    for unit, way in ((2, 0), (3, 0), (0, 1), (1, 1)):
        wq_send(unit, way).wait_recv()
    for unit, way in ((0, 0), (2, 1), (1, 0), (3, 1)):
        wq_pass(unit, way).wait_recv()

    def mid_wait(i, c):
        mid_copy(i).wait_recv()
        return c

    lax.fori_loop(1, NT, mid_wait, 0)
    middle = midr[...].reshape(NT * PART, D).astype(F32)
    centred = middle - jnp.mean(middle, axis=-1, keepdims=True)
    variance = jnp.mean(centred * centred, axis=-1, keepdims=True)
    normed = (centred * lax.rsqrt(variance + 1e-06) * (1.0 + sc_ref[...]) + sh_ref[...]).astype(BF16)

    tokens = NT * PART
    same = (lax.broadcasted_iota(jnp.int32, (tokens, tokens), 0) % PART) == (
        lax.broadcasted_iota(jnp.int32, (tokens, tokens), 1) % PART
    )

    def heads(j, c):
        proj = lax.dot_general(
            wq[j].reshape(3 * 144, D), normed, (((1,), (1,)), ((), ())), preferred_element_type=F32
        )
        for e in range(2):
            tq = proj[HD * e : HD * (e + 1)].astype(BF16)
            tk = proj[144 + HD * e : 144 + HD * (e + 1)].T.astype(BF16)
            tv = proj[288 + HD * e : 288 + HD * (e + 1)].astype(BF16)
            s = jnp.dot(tk, tq, preferred_element_type=F32) * FACTOR
            s = jnp.where(same, s, -jnp.inf)
            p = jnp.exp(s - jnp.max(s, axis=0, keepdims=True))
            p = (p / jnp.sum(p, axis=0, keepdims=True)).astype(BF16)
            mixt[pl.ds(pl.multiple_of(144 * j + HD * e, 8), HD), :] = jnp.dot(tv, p, preferred_element_type=F32)
        return c

    lax.fori_loop(0, 4, heads, 0)
    mixed = mixt[...].T.astype(BF16)
    summed = jnp.dot(mixed, wo[...].reshape(576, D), preferred_element_type=F32)
    keep = jnp.where(xh == 0, 1.0, 0.0).astype(F32)
    part = keep * midr[...].reshape(tokens, D).astype(F32) + gt_ref[...] * summed
    fins[...] = part.astype(BF16).reshape(NT, PART, D)

    def fin_copy(f):
        return remote(fins.at[f], finr.at[t], sf.at[f], rf.at[t], {"section": nxt, "tm": f})

    def fin_start(f, c):
        fin_copy(f).start()
        return c

    lax.fori_loop(0, NT, fin_start, 0)

    def fin_wait(f, c):
        remote(fins.at[f], finr.at[f], sf.at[f], rf.at[f], {"section": nxt, "tm": f}).wait_recv()
        return c

    lax.fori_loop(0, NT, fin_wait, 0)
    for j in range(4):
        out_ref[PART * j : PART * (j + 1), :] = (finr[2 * j].astype(F32) + finr[2 * j + 1].astype(F32)).astype(BF16)

    def left_z(i, c):
        kv_copy(i).wait_send()
        q_copy(i).wait_send()
        o_copy(i).wait_send()
        return c

    lax.fori_loop(1, NZ, left_z, 0)

    def left_ring(j, c):
        ring_right(j).wait_send()
        ring_left(j).wait_send()
        return c

    lax.fori_loop(0, 7, left_ring, 0)
    ring_right_half().wait_send()
    ring_left_half().wait_send()
    for way in range(2):
        wy_copy(way).wait_send()
        wy_pass(way).wait_send()
        for unit in range(4):
            wq_send(unit, way).wait_send()
    for i, tt in ((0, t), (1, t_yl), (2, t_yr), (3, t_y2)):
        wx_copy(i, tt).wait_send()
    for unit, way in ((0, 0), (2, 1), (1, 0), (3, 1)):
        wq_pass(unit, way).wait_send()

    def left_t(i, c):
        mid_copy(i).wait_send()
        return c

    lax.fori_loop(1, NT, left_t, 0)

    def left_f(f, c):
        fin_copy(f).wait_send()
        return c

    lax.fori_loop(0, NT, left_f, 0)


def shards(
    hidden_in, query_s, key_s, value_s, out_proj_s, gate_s, shift_t, scale_t, qkv_t, out_t, gate_t
):
    vm = pl.BlockSpec(memory_space=pltpu.VMEM)
    hbm = pl.BlockSpec(memory_space=pl.ANY)
    dma = pltpu.SemaphoreType.DMA
    plane = (HD, ROWS)
    out = pl.pallas_call(
        kernel,
        out_shape=jax.ShapeDtypeStruct((ROWS, D), BF16),
        in_specs=[vm, vm, vm, hbm, vm, vm, vm, vm, hbm, hbm, vm],
        out_specs=vm,
        scratch_shapes=[
            pltpu.VMEM((NZ, 2 * HD, ROWS), BF16),
            pltpu.VMEM((NZ, 2 * HD, ROWS), BF16),
            pltpu.VMEM((NZ, *plane), BF16),
            pltpu.VMEM((NZ, *plane), BF16),
            pltpu.VMEM((NZ, *plane), BF16),
            pltpu.VMEM((NZ, *plane), BF16),
            pltpu.VMEM((NZ, 2, *plane), BF16),
            pltpu.VMEM((NT, NZ, *plane), BF16),
            pltpu.VMEM((D, D), BF16),
            pltpu.VMEM((NZ * ROWS, HD), BF16),
            pltpu.VMEM((HD + 8, NZ * ROWS), BF16),
            pltpu.VMEM((D, ROWS), F32),
            pltpu.VMEM((4, 3, 144, D), BF16),
            pltpu.VMEM((4, 144, D), BF16),
            pltpu.VMEM((ROWS, D), BF16),
            pltpu.VMEM((ROWS, D), BF16),
            pltpu.VMEM((NT, PART, D), BF16),
            pltpu.VMEM((576, NT * PART), F32),
            pltpu.VMEM((NT, PART, D), BF16),
            pltpu.VMEM((NT, PART, D), BF16),
            dma((NZ,)), dma((NZ,)), dma((NZ,)), dma((NZ,)), dma((NZ,)), dma((NZ,)),
            dma((2, 8)), dma((2, 8)), dma((4,)), dma((4,)), dma((4,)), dma((4,)),
            dma((2, 8)), dma((2, 8)), dma((NT,)), dma((NT,)), dma((NT,)), dma((NT,)), dma((3,)),
        ],
        compiler_params=pltpu.CompilerParams(
            collective_id=0, has_side_effects=True, vmem_limit_bytes=56 * 1024 * 1024
        ),
        cost_estimate=pl.CostEstimate(flops=3_000_000_000, bytes_accessed=6_000_000, transcendentals=4_500_000),
        name="st_block_pair",
    )(
        query_s[0, 0], key_s[0, 0], value_s[0, 0], hidden_in[0, 0], out_proj_s[0],
        gate_s, shift_t, scale_t, qkv_t[0], out_t[0], gate_t,
    )
    return out[None, None]


def solution(mesh):
    in_specs = (
        P("section", "tm", "space", None),
        P("section", "tm", "space", None),
        P("section", "tm", "space", None),
        P("section", "tm", "space", None),
        P("section", "space", None),
        P("section", None),
        P("section", None),
        P("section", None),
        P("section", None, "tm", None),
        P("section", "tm", None),
        P("section", None),
    )
    out_specs = P("section", "tm", "space", None)
    return jax.shard_map(shards, mesh=mesh, in_specs=in_specs, out_specs=out_specs, check_vma=False)
```

time: 410 us -> 131 us (0.32)
  waiting for transfers between devices: 274 us -> 0 us
  Pallas kernels: 0 us -> 129 us
  local copies, waits for them, and re-layouts: 67 us -> 1.7 us
  matrix products: 40.8 us -> 0 us
  between operations: 13.3 us -> 0.01 us
  other arithmetic: 6.79 us -> 0 us
  starting transfers between devices: 6.74 us -> 0 us
    all_gather x5 -> x0, waiting for transfers between devices: 267 us -> none  [the longest x1 76.2 us: shards(): lax.all_gather(normed.reshape(frames, patches, width), 'tm', axis=0, tile...]
    pallas_call x0 -> x1, Pallas kernels: none -> 129 us  [shards(): pl.pallas_call(kernel, out_shape=jax.ShapeDtypeStruct((ROWS, D), BF16), i...]
    dot_general x13 -> x0, matrix products: 40.8 us -> none  [the longest x4 16.2 us: absorb_keys(): jnp.einsum('fqhd,fkhd->fhqk', queries_split, keys_block, preferred_elemen...]
    another operation x2 -> x0, local copies, waits for them, and re-layouts: 34.8 us -> none  [the longest x1 17.4 us: keyed_attention(): jnp.moveaxis(key_rows.reshape(frames, blocks, 512, HEADS, head_dim), 1, 0)]
    unnamed x10 -> x1, local copies, waits for them, and re-layouts: 28.2 us -> 1.7 us
  transfers between devices with their start and end apart: 7 -> 0, of which waited for: 6 -> 0; matrix products, arithmetic and copies ran while one was open for 26% -> 0% of each run, Pallas kernels for 0% -> 0%
where the time goes in v1:
time: 131 us; the launch traced here: 130 us
  Pallas kernels  129 us (98%)
  local copies, waits for them, and re-layouts  1.7 us (1%)
    pallas_call x1, Pallas kernels, shards(): pl.pallas_call(kernel, out_shape=jax.ShapeDtypeStruct((ROWS, D), BF16), i...  129 us

profile of v1, /device:TPU:1, one launch (start us, length us, event | category | flops | bytes accessed | tf_op | source)
XLA Modules:
  0.0 130.2 jit_solution(10821690431447457714)
XLA Ops:
  0.0 128.5 %st_block_pair.1 = bf16[128,1152]{1,0:T(8,128)(2,1)} custom-call(bf16[128,1152]{1,0:T(8,128)(2,1)} %bitcast.11, bf16[128,1152]{1,0:T(8,128)(2,1)} %bitcast.12, bf16[128,1152]{1,0:T(8,128)(2,1)} %bitcast.13, bf16[128,1152]{1,0:T(8,128)(2,1)} %bitcast.14, bf16[72,1152]{1,0:T(8,128)(2,1)} %bitcast.15, f32[1,1152]{1,0:T(1,128)} %gs_ref.1, f32[1,1152]{1,0:T(1,128)} %sh_ref.1, ...), custom_call_target="tpu_custom_call" | custom-call | flops 3000000000 | bytes 6000000 | tf_op jit(solution)/shard_map/st_block_pair/pallas_call | solution.py:395
  128.5 1.7 %copy.13 = bf16[1,1,128,1152]{3,2,1,0:T(8,128)(2,1)} copy(bf16[1,1,128,1152]{3,2,1,0:T(8,128)(2,1)} %bitcast.8) | data formatting | bytes 589824

commit v2 on v1

--- a/solution.py
+++ b/solution.py
@@ -16,12 +16,13 @@
 ROWS = 128
 PART = 32
 FACTOR = HD ** (-0.5)
+FACTOR2 = FACTOR * 1.4426950408889634
 
 
 def kernel(
-    q_ref, k_ref, v_ref, hid_hbm, w_ref, gs_ref, sh_ref, sc_ref, qkv_hbm, ot_hbm, gt_ref,
-    out_ref,
-    kvs, kvr, qs, qr, osd, orc, wz, wt, wfull, kmat, vmat, ofull, wq, wo, hid, mids, midr, mixt, fins, finr,
+    q_hbm, k_hbm, v_hbm, hid_hbm, w_hbm, gs_ref, sh_ref, sc_ref, qkv_hbm, ot_hbm, gt_ref,
+    finr,
+    q_ref, k_ref, v_ref, w_ref, kvs, kvr, qs, qr, osd, orc, wz, wall, acc, kmat, vmat, wq, wo, hid, mids, midr, mixt, fins,
     skv, rkv, sq, rq, so, ro, sw, rw, swy, rwy, swx, rwx, sqy, rqy, sm, rm, sf, rf, loc,
 ):
     sec = lax.axis_index("section")
@@ -69,6 +70,12 @@
 
     lax.fori_loop(0, NT, greet_s, 0)
 
+    loc_in = [
+        pltpu.make_async_copy(a, b, loc.at[3 + i])
+        for i, (a, b) in enumerate(((k_hbm, k_ref), (v_hbm, v_ref), (q_hbm, q_ref), (w_hbm, w_ref)))
+    ]
+    for c in loc_in:
+        c.start()
     loc_q = pltpu.make_async_copy(qkv_hbm, wq.at[y], loc.at[0])
     loc_o = pltpu.make_async_copy(ot_hbm, wo.at[y], loc.at[1])
     loc_h = pltpu.make_async_copy(hid_hbm, hid, loc.at[2])
@@ -76,6 +83,8 @@
     loc_o.start()
     loc_h.start()
 
+    for c in loc_in:
+        c.wait()
     wz[z, 0] = w_ref[:, pl.ds(pl.multiple_of(t * 128, 128), 128)]
     wz[z, 1] = w_ref[:, 1024:1152]
     kt = k_ref[...].astype(F32).T
@@ -127,48 +136,13 @@
         to = (z + i) % NZ
         return remote(qs.at[to], qr.at[z], sq.at[i], rq.at[i], {"space": to})
 
-    def kv_start(i, c):
+    def kv_start(i):
         kv_copy(NZ - i).start()
         kv_copy(i).start()
-        return c
-
-    lax.fori_loop(1, 8, kv_start, 0)
-    kv_copy(8).start()
-
-    def q_start(i, c):
+
+    def q_start(i):
         q_copy(i).start()
         q_copy(NZ - i).start()
-        return c
-
-    lax.fori_loop(1, 8, q_start, 0)
-    q_copy(8).start()
-
-    def ring_step(j, c):
-        ring_right(j - 1).wait_recv()
-        ring_right(j).start()
-        ring_left(j - 1).wait_recv()
-        ring_left(j).start()
-        return c
-
-    lax.fori_loop(1, 7, ring_step, 0)
-    ring_right(6).wait_recv()
-    ring_right_half().start()
-    ring_left(6).wait_recv()
-    ring_left_half().start()
-    ring_right_half().wait_recv()
-    ring_left_half().wait_recv()
-
-    wt[t] = wz[:, 0]
-
-    def wy_copy(way):
-        return remote(wt.at[t], wt.at[t], swy.at[way], rwy.at[way], yr if way == 0 else yl)
-
-    def wx_copy(i, tt):
-        return remote(wt.at[tt], wt.at[tt], swx.at[i], rwx.at[i], xo)
-
-    wy_copy(0).start()
-    wy_copy(1).start()
-    wx_copy(0, t).start()
 
     def take_kv(src):
         block = kvr[src].astype(F32)
@@ -176,15 +150,64 @@
         kmat[off, :] = block[:HD].T.astype(BF16)
         vmat[:HD, off] = block[HD:].astype(BF16)
 
-    vmat[HD:, :] = jnp.ones((8, NZ * ROWS), BF16)
-    take_kv(z)
-
     def kv_take(i, c):
         kv_copy(i).wait_recv()
         take_kv((z + NZ - i) % NZ)
-        return c
-
-    lax.fori_loop(1, NZ, kv_take, 0)
+        kv_copy(NZ - i).wait_recv()
+        take_kv((z + i) % NZ)
+        return c
+
+    kv_start(1)
+    kv_start(2)
+    kv_start(3)
+    vmat[HD:, :] = jnp.ones((8, NZ * ROWS), BF16)
+    take_kv(z)
+    for j in range(1, 7):
+        if j < 5:
+            kv_start(j + 3)
+        elif j == 5:
+            kv_copy(8).start()
+            q_start(1)
+        else:
+            q_start(2)
+            q_start(3)
+        ring_right(j - 1).wait_recv()
+        ring_right(j).start()
+        ring_left(j - 1).wait_recv()
+        ring_left(j).start()
+        if j > 2:
+            kv_take(j - 2, 0)
+    ring_right(6).wait_recv()
+    ring_right_half().start()
+    ring_left(6).wait_recv()
+    ring_left_half().start()
+    q_start(4)
+    q_start(5)
+    ring_right_half().wait_recv()
+    ring_left_half().wait_recv()
+
+    def columns(tt):
+        return wall.at[:, :, pl.ds(pl.multiple_of(tt * 128, 128), 128)]
+
+    wall[:, :, pl.ds(pl.multiple_of(t * 128, 128), 128)] = wz[:, 0]
+    wall[:, :, 1024:1152] = wz[:, 1]
+
+    def wy_copy(way):
+        return remote(columns(t), columns(t), swy.at[way], rwy.at[way], yr if way == 0 else yl)
+
+    def wx_copy(i, tt):
+        return remote(columns(tt), columns(tt), swx.at[i], rwx.at[i], xo)
+
+    wy_copy(0).start()
+    wy_copy(1).start()
+    wx_copy(0, t).start()
+    q_start(6)
+    q_start(7)
+    q_copy(8).start()
+
+    lax.fori_loop(5, 8, kv_take, 0)
+    kv_copy(8).wait_recv()
+    take_kv((z + 8) % NZ)
 
     def wq_pass(unit, way):
         dev, yy = (yr, y_l) if way == 0 else (yl, y_r)
@@ -194,7 +217,7 @@
 
     def wy_pass(way):
         dev, tt = (yr, t_yl) if way == 0 else (yl, t_yr)
-        part = wt.at[tt, pl.ds(8 * way, 8)]
+        part = wall.at[pl.ds(8 * way, 8), :, pl.ds(pl.multiple_of(tt * 128, 128), 128)]
         return remote(part, part, swy.at[2 + way], rwy.at[2 + way], dev)
 
     wy_copy(0).wait_recv()
@@ -223,7 +246,7 @@
         queries = jnp.concatenate([qr[src_a], qr[src_b]], axis=1)
         s = jnp.dot(kmat[...], queries, preferred_element_type=F32)
         top = jnp.max(s, axis=0, keepdims=True)
-        p = jnp.exp((s - top) * FACTOR).astype(BF16)
+        p = jnp.exp2((s - top) * FACTOR2).astype(BF16)
         o = jnp.dot(vmat[...], p, preferred_element_type=F32)
         o = (o[:HD] / o[HD : HD + 1]).astype(BF16)
         osd[src_a] = o[:, :ROWS]
@@ -248,29 +271,20 @@
     for i, tt in ((0, t), (1, t_yl), (2, t_yr), (3, t_y2)):
         wx_copy(i, tt).wait_recv()
 
-    def w_rows(j, c):
-        row = pl.ds(pl.multiple_of(144 * j, 144), 144)
-        for b in range(9):
-            if b < 8:
-                lo, hi = wt[b, 2 * j], wt[b, 2 * j + 1]
-            else:
-                lo, hi = wz[2 * j, 1], wz[2 * j + 1, 1]
-            wfull[row, 128 * b : 128 * (b + 1)] = jnp.concatenate([lo.astype(F32), hi.astype(F32)], axis=0).astype(BF16)
-        return c
-
-    lax.fori_loop(0, 8, w_rows, 0)
+    def project(src):
+        return jnp.dot(orc[src].astype(F32).T.astype(BF16), wall[src], preferred_element_type=F32)
+
+    def o_take(d, c):
+        o_copy(d).wait_recv()
+        o_copy(NZ - d).wait_recv()
+        acc[...] += project((z + NZ - d) % NZ) + project((z + d) % NZ)
+        return c
+
+    acc[...] = project(z)
+    lax.fori_loop(1, 8, o_take, 0)
+    o_copy(8).wait_recv()
     loc_h.wait()
-
-    def o_take(i, c):
-        o_copy(i).wait_recv()
-        src = (z + NZ - i) % NZ
-        ofull[pl.ds(pl.multiple_of(src * HD, 8), HD), :] = orc[src].astype(F32)
-        return c
-
-    ofull[pl.ds(pl.multiple_of(z * HD, 8), HD), :] = orc[z].astype(F32)
-    lax.fori_loop(1, NZ, o_take, 0)
-    attended = ofull[...].T.astype(BF16)
-    projected = jnp.dot(attended, wfull[...], preferred_element_type=F32)
+    projected = acc[...] + project((z + 8) % NZ)
     mids[...] = (hid[...].astype(F32) + gs_ref[...] * projected).astype(BF16)
 
     def mid_copy(i):
@@ -324,28 +338,24 @@
 
     lax.fori_loop(0, 4, heads, 0)
     mixed = mixt[...].T.astype(BF16)
-    summed = jnp.dot(mixed, wo[...].reshape(576, D), preferred_element_type=F32)
     keep = jnp.where(xh == 0, 1.0, 0.0).astype(F32)
-    part = keep * midr[...].reshape(tokens, D).astype(F32) + gt_ref[...] * summed
-    fins[...] = part.astype(BF16).reshape(NT, PART, D)
 
     def fin_copy(f):
         return remote(fins.at[f], finr.at[t], sf.at[f], rf.at[t], {"section": nxt, "tm": f})
 
-    def fin_start(f, c):
-        fin_copy(f).start()
-        return c
-
-    lax.fori_loop(0, NT, fin_start, 0)
+    for half in range(2):
+        rows = slice(128 * half, 128 * (half + 1))
+        summed = jnp.dot(mixed[rows], wo[...].reshape(576, D), preferred_element_type=F32)
+        part = keep * midr[4 * half : 4 * (half + 1)].reshape(128, D).astype(F32) + gt_ref[...] * summed
+        fins[4 * half : 4 * (half + 1)] = part.astype(BF16).reshape(4, PART, D)
+        for f in range(4 * half, 4 * (half + 1)):
+            fin_copy(f).start()
 
     def fin_wait(f, c):
         remote(fins.at[f], finr.at[f], sf.at[f], rf.at[f], {"section": nxt, "tm": f}).wait_recv()
         return c
 
     lax.fori_loop(0, NT, fin_wait, 0)
-    for j in range(4):
-        out_ref[PART * j : PART * (j + 1), :] = (finr[2 * j].astype(F32) + finr[2 * j + 1].astype(F32)).astype(BF16)
-
     def left_z(i, c):
         kv_copy(i).wait_send()
         q_copy(i).wait_send()
@@ -394,10 +404,14 @@
     plane = (HD, ROWS)
     out = pl.pallas_call(
         kernel,
-        out_shape=jax.ShapeDtypeStruct((ROWS, D), BF16),
-        in_specs=[vm, vm, vm, hbm, vm, vm, vm, vm, hbm, hbm, vm],
-        out_specs=vm,
+        out_shape=jax.ShapeDtypeStruct((NT, PART, D), BF16),
+        in_specs=[hbm, hbm, hbm, hbm, hbm, vm, vm, vm, hbm, hbm, vm],
+        out_specs=hbm,
         scratch_shapes=[
+            pltpu.VMEM((ROWS, D), BF16),
+            pltpu.VMEM((ROWS, D), BF16),
+            pltpu.VMEM((ROWS, D), BF16),
+            pltpu.VMEM((HD, D), BF16),
             pltpu.VMEM((NZ, 2 * HD, ROWS), BF16),
             pltpu.VMEM((NZ, 2 * HD, ROWS), BF16),
             pltpu.VMEM((NZ, *plane), BF16),
@@ -405,11 +419,10 @@
             pltpu.VMEM((NZ, *plane), BF16),
             pltpu.VMEM((NZ, *plane), BF16),
             pltpu.VMEM((NZ, 2, *plane), BF16),
-            pltpu.VMEM((NT, NZ, *plane), BF16),
-            pltpu.VMEM((D, D), BF16),
+            pltpu.VMEM((NZ, HD, D), BF16),
+            pltpu.VMEM((ROWS, D), F32),
             pltpu.VMEM((NZ * ROWS, HD), BF16),
             pltpu.VMEM((HD + 8, NZ * ROWS), BF16),
-            pltpu.VMEM((D, ROWS), F32),
             pltpu.VMEM((4, 3, 144, D), BF16),
             pltpu.VMEM((4, 144, D), BF16),
             pltpu.VMEM((ROWS, D), BF16),
@@ -417,10 +430,9 @@
             pltpu.VMEM((NT, PART, D), BF16),
             pltpu.VMEM((576, NT * PART), F32),
             pltpu.VMEM((NT, PART, D), BF16),
-            pltpu.VMEM((NT, PART, D), BF16),
             dma((NZ,)), dma((NZ,)), dma((NZ,)), dma((NZ,)), dma((NZ,)), dma((NZ,)),
             dma((2, 8)), dma((2, 8)), dma((4,)), dma((4,)), dma((4,)), dma((4,)),
-            dma((2, 8)), dma((2, 8)), dma((NT,)), dma((NT,)), dma((NT,)), dma((NT,)), dma((3,)),
+            dma((2, 8)), dma((2, 8)), dma((NT,)), dma((NT,)), dma((NT,)), dma((NT,)), dma((7,)),
         ],
         compiler_params=pltpu.CompilerParams(
             collective_id=0, has_side_effects=True, vmem_limit_bytes=56 * 1024 * 1024
@@ -431,7 +443,8 @@
         query_s[0, 0], key_s[0, 0], value_s[0, 0], hidden_in[0, 0], out_proj_s[0],
         gate_s, shift_t, scale_t, qkv_t[0], out_t[0], gate_t,
     )
-    return out[None, None]
+    halves = out.reshape(4, 2, PART, D).astype(F32)
+    return (halves[:, 0] + halves[:, 1]).astype(BF16).reshape(1, 1, ROWS, D)
 
 
 def solution(mesh):

time: 131 us -> 117 us (0.89)
  Pallas kernels: 129 us -> 115 us
  other arithmetic: 0 us -> 1.92 us
  local copies, waits for them, and re-layouts: 1.7 us -> 0 us
    pallas_call x1, Pallas kernels: 129 us -> 115 us  [shards(): pl.pallas_call(kernel, out_shape=jax.ShapeDtypeStruct((NT, PART, D), BF16...]
    convert_element_type x0 -> x2, other arithmetic: none -> 1.92 us  [the longest x1 1.15 us: shards(): halves = out.reshape(4, 2, PART, D).astype(F32)]
    unnamed x1 -> x0, local copies, waits for them, and re-layouts: 1.7 us -> none
where the time goes in v2:
time: 117 us; the launch traced here: 116 us
  Pallas kernels  115 us (98%)
  other arithmetic  1.92 us (2%)
    pallas_call x1, Pallas kernels, shards(): pl.pallas_call(kernel, out_shape=jax.ShapeDtypeStruct((NT, PART, D), BF16...  115 us

profile of v2, /device:TPU:1, one launch (start us, length us, event | category | flops | bytes accessed | tf_op | source)
XLA Modules:
  0.0 116.5 jit_solution(3745866442178924323)
XLA Ops:
  0.0 114.5 %st_block_pair.1 = bf16[8,32,1152]{2,1,0:T(8,128)(2,1)} custom-call(bf16[128,1152]{1,0:T(8,128)(2,1)} %bitcast.13, bf16[128,1152]{1,0:T(8,128)(2,1)} %bitcast.14, bf16[128,1152]{1,0:T(8,128)(2,1)} %bitcast.15, bf16[128,1152]{1,0:T(8,128)(2,1)} %bitcast.16, bf16[72,1152]{1,0:T(8,128)(2,1)} %bitcast.17, f32[1,1152]{1,0:T(1,128)} %gs_ref.1, f32[1,1152]{1,0:T(1,128)} %sh_ref.1, ...), custom_call_target="tpu_custom_call" | custom-call | flops 3000000000 | bytes 6000000 | tf_op jit(solution)/shard_map/st_block_pair/pallas_call | solution.py:405
  114.5 1.1 convert.1
  115.7 0.8 fusion

commit v3 on v2

v3 whole, which is shorter than its diff:
```python
import jax
import jax.numpy as jnp
from jax import lax
from jax.experimental import pallas as pl
from jax.experimental.pallas import tpu as pltpu
from jax.sharding import PartitionSpec as P

MESH = pl.DeviceIdType.MESH
F32 = jnp.float32
BF16 = jnp.bfloat16
D = 1152
HD = 72
NZ = 16
NT = 8
NS = 4
ROWS = 128
PART = 32
HALF = 16
PACE = (2, 1)
KV1 = 5
FACTOR = HD ** (-0.5)
FACTOR2 = FACTOR * 1.4426950408889634


def kernel(
    q_hbm, k_hbm, v_hbm, hid_hbm, w_hbm, gs_ref, sh_ref, sc_ref, qkv_hbm, ot_hbm, gt_ref,
    finr,
    q_ref, k_ref, v_ref, w_ref, kvs, kvr, qs, qr, osd, orc, wpad, ws, wall, acc, kmat, vmat, wq, wo, hid, mids, midr, proj, mixt, fins,
    skv, rkv, sq, rq, so, ro, swz, rwz, swy, rwy, swx, rwx, sqy, rqy, sm, rm, sf, rf, loc,
):
    sec = lax.axis_index("section")
    t = lax.axis_index("tm")
    z = lax.axis_index("space")
    y = t // 2
    xh = t % 2
    nxt = (sec + 1) % NS
    prv = (sec + NS - 1) % NS
    zr = {"space": (z + 1) % NZ}
    zl = {"space": (z + NZ - 1) % NZ}
    yr = {"tm": (t + 2) % NT}
    yl = {"tm": (t + NT - 2) % NT}
    xo = {"tm": t + 1 - 2 * xh}
    t_yr = (t + 2) % NT
    t_yl = (t + NT - 2) % NT
    t_y2 = (t + 4) % NT
    y_r = (y + 1) % 4
    y_l = (y + 3) % 4

    def remote(src, dst, s_sem, r_sem, dev):
        return pltpu.make_async_remote_copy(
            src_ref=src, dst_ref=dst, send_sem=s_sem, recv_sem=r_sem, device_id=dev, device_id_type=MESH
        )

    barrier = pltpu.get_barrier_semaphore()

    def greet_z(i, c):
        pl.semaphore_signal(barrier, inc=1, device_id={"space": (z + i) % NZ}, device_id_type=MESH)
        return c

    lax.fori_loop(1, NZ, greet_z, 0)

    def greet_t(i, c):
        pl.semaphore_signal(barrier, inc=1, device_id={"tm": (t + i) % NT}, device_id_type=MESH)
        return c

    lax.fori_loop(1, NT, greet_t, 0)

    def greet_s(i, c):
        pl.semaphore_signal(barrier, inc=1, device_id={"section": nxt, "tm": i}, device_id_type=MESH)
        pl.semaphore_signal(barrier, inc=1, device_id={"section": prv, "tm": i}, device_id_type=MESH)
        return c

    lax.fori_loop(0, NT, greet_s, 0)

    loc_in = [
        pltpu.make_async_copy(a, b, loc.at[3 + i])
        for i, (a, b) in enumerate(((k_hbm, k_ref), (v_hbm, v_ref), (q_hbm, q_ref), (w_hbm, w_ref)))
    ]
    for c in loc_in:
        c.start()
    loc_q = pltpu.make_async_copy(qkv_hbm, wq.at[y], loc.at[0])
    loc_o = pltpu.make_async_copy(ot_hbm, wo.at[y], loc.at[1])
    loc_h = pltpu.make_async_copy(hid_hbm, hid, loc.at[2])
    loc_q.start()
    loc_o.start()
    loc_h.start()

    for c in loc_in:
        c.wait()
    wpad[...] = jnp.concatenate([w_ref[:, 1024:1152].astype(F32), jnp.zeros((8, 128), F32)], axis=0).astype(BF16)
    ws[t, 0, 0, :16] = wpad[pl.ds(pl.multiple_of((t % 5) * 16, 16), 16), :]
    ws[t, 0, 0, 16:] = w_ref[:, pl.ds(pl.multiple_of(t * 128, 128), 128)]
    kt = k_ref[...].astype(F32).T
    vt = v_ref[...].astype(F32).T
    for h in range(NZ):
        kvs[h] = jnp.concatenate([kt[HD * h : HD * (h + 1)], vt[HD * h : HD * (h + 1)]], axis=0).astype(BF16)
    qt = q_ref[...].astype(F32).T
    for h in range(NZ):
        qs[h] = qt[HD * h : HD * (h + 1)].astype(BF16)
    kvr[z] = kvs[z]
    qr[z] = qs[z]

    pl.semaphore_wait(barrier, (NZ - 1) + (NT - 1) + 2 * NT)

    def wz_far(k):
        return remote(ws.at[t, 0, 0], ws.at[t, 0, 4 - k], swz.at[k], rwz.at[k], {"space": (z + 4 * k) % NZ})

    def wz_near(i):
        to, src, dst = (
            ((z + NZ - 1) % NZ, ws.at[t, 0], ws.at[t, 1]),
            ((z + 1) % NZ, ws.at[t, 0], ws.at[t, 3]),
            ((z + NZ - 2) % NZ, ws.at[t, 0, pl.ds(2, 2)], ws.at[t, 2, pl.ds(2, 2)]),
            ((z + 2) % NZ, ws.at[t, 0, pl.ds(1, 2)], ws.at[t, 2, pl.ds(0, 2)]),
        )[i]
        return remote(src, dst, swz.at[4 + i], rwz.at[4 + i], {"space": to})

    for k in (2, 1, 3):
        wz_far(k).start()

    def wq_send(unit, way):
        dev = yr if way == 0 else yl
        if unit < 3:
            return remote(qkv_hbm.at[unit], wq.at[y, unit], sqy.at[way, unit], rqy.at[way, unit], dev)
        return remote(ot_hbm, wo.at[y], sqy.at[way, 3], rqy.at[way, 3], dev)

    for unit in (0, 1, 2, 3):
        wq_send(unit, 0).start()
        wq_send((unit + 2) % 4, 1).start()

    def kv_copy(i):
        to = (z + i) % NZ
        return remote(kvs.at[to], kvr.at[z], skv.at[i], rkv.at[i], {"space": to})

    def q_copy(i):
        to = (z + i) % NZ
        return remote(qs.at[to], qr.at[z], sq.at[i], rq.at[i], {"space": to})

    def kv_start(i):
        kv_copy(NZ - i).start()
        kv_copy(i).start()

    def one(copy):
        copy(8).start()

    def q_start(i):
        q_copy(i).start()
        q_copy(NZ - i).start()

    def take_kv(src):
        block = kvr[src].astype(F32)
        off = pl.ds(pl.multiple_of(src * ROWS, ROWS), ROWS)
        kmat[off, :] = block[:HD].T.astype(BF16)
        vmat[:HD, off] = block[HD:].astype(BF16)

    def kv_take(i, c):
        kv_copy(i).wait_recv()
        take_kv((z + NZ - i) % NZ)
        kv_copy(NZ - i).wait_recv()
        take_kv((z + i) % NZ)
        return c

    def wy_copy(way):
        return remote(ws.at[t], ws.at[t], swy.at[way], rwy.at[way], yr if way == 0 else yl)

    def wy_pass(way):
        dev, tt = (yr, t_yl) if way == 0 else (yl, t_yr)
        part = ws.at[tt, pl.ds(2 * way, 2)]
        return remote(part, part, swy.at[2 + way], rwy.at[2 + way], dev)

    def wx_copy(i):
        part = ws.at[(t, t_yl, t_yr, t_y2)[i]]
        return remote(part, part, swx.at[i], rwx.at[i], xo)

    queue = [(one, kv_copy)] + [(kv_start, i) for i in range(7, 0, -1)] + [(one, q_copy)] + [(q_start, i) for i in range(7, 0, -1)]

    def issue(count):
        for _ in range(count):
            start, what = queue.pop(0)
            start(what)

    issue(PACE[0])
    vmat[HD:, :] = jnp.ones((8, NZ * ROWS), BF16)
    take_kv(z)
    for k in (1, 3, 2):
        wz_far(k).wait_recv()
    for i in range(4):
        wz_near(i).start()
    issue(PACE[1])
    for i in range(4):
        wz_near(i).wait_recv()
    wx_copy(0).start()
    wy_copy(0).start()
    wy_copy(1).start()
    issue(len(queue))

    kv_copy(8).wait_recv()
    take_kv((z + 8) % NZ)
    lax.fori_loop(1, KV1, lambda i, c: kv_take(8 - i, c), 0)
    wy_copy(0).wait_recv()
    wy_pass(0).start()
    wx_copy(1).start()
    wy_copy(1).wait_recv()
    wy_pass(1).start()
    wx_copy(2).start()
    lax.fori_loop(KV1, 8, lambda i, c: kv_take(8 - i, c), 0)

    def wq_pass(unit, way):
        dev, yy = (yr, y_l) if way == 0 else (yl, y_r)
        if unit < 3:
            return remote(wq.at[yy, unit], wq.at[yy, unit], sqy.at[way, 4 + unit], rqy.at[way, 4 + unit], dev)
        return remote(wo.at[yy], wo.at[yy], sqy.at[way, 7], rqy.at[way, 7], dev)

    def o_copy(i):
        to = (z + i) % NZ
        return remote(osd.at[to], orc.at[z], so.at[i], ro.at[i], {"space": to})

    def attend(i, c):
        d = 8 - i
        src_a = (z + NZ - d) % NZ
        src_b = jnp.where(d == 8, z, (z + d) % NZ)
        q_copy(d).wait_recv()

        @pl.when(d < 8)
        def _():
            q_copy(NZ - d).wait_recv()

        queries = jnp.concatenate([qr[src_a], qr[src_b]], axis=1)
        s = jnp.dot(kmat[...], queries, preferred_element_type=F32)
        top = jnp.max(s, axis=0, keepdims=True)
        p = jnp.exp2((s - top) * FACTOR2).astype(BF16)
        o = jnp.dot(vmat[...], p, preferred_element_type=F32)
        o = (o[:HD] / o[HD : HD + 1]).astype(BF16)
        osd[src_a] = o[:, :ROWS]
        osd[src_b] = o[:, ROWS:]
        o_copy(NZ - d).start()

        @pl.when(d < 8)
        def _():
            o_copy(d).start()

        @pl.when(i == 1)
        def _():
            wy_pass(0).wait_recv()
            wy_pass(1).wait_recv()
            wx_copy(3).start()

        @pl.when(i == 4)
        def _():
            for unit, way in ((0, 0), (2, 1), (1, 0), (3, 1)):
                wq_send(unit, way).wait_recv()
                wq_pass(unit, way).start()

        return c

    lax.fori_loop(0, 8, attend, 0)
    orc[z] = osd[z]

    for i in range(4):
        wx_copy(i).wait_recv()

    def w_rows(i, c):
        m, k = i // 4, i % 4
        for b in range(8):
            wall[i, :, 128 * b : 128 * (b + 1)] = ws[b, m, k, 16:]
        last = [ws[b, m, k, :16].astype(F32) for b in range(5)]
        wall[i, :, 1024:] = jnp.concatenate(last, axis=0)[:HD].astype(BF16)
        return c

    lax.fori_loop(0, NZ, w_rows, 0)

    def project(r):
        slot = (r % 4) * 4 + ((r + 1) // 4) % 4
        return jnp.dot(orc[(z + r) % NZ].astype(F32).T.astype(BF16), wall[slot], preferred_element_type=F32)

    def o_take(i, c):
        d = 8 - i
        o_copy(d).wait_recv()
        o_copy(NZ - d).wait_recv()
        acc[...] += project(NZ - d) + project(d)
        return c

    acc[...] = project(0)
    o_copy(8).wait_recv()
    acc[...] += project(8)
    lax.fori_loop(1, 7, o_take, 0)
    o_copy(1).wait_recv()
    o_copy(NZ - 1).wait_recv()
    loc_h.wait()
    projected = acc[...] + project(NZ - 1) + project(1)
    mids[...] = (hid[...].astype(F32) + gs_ref[...] * projected).astype(BF16)

    def mid_copy(i, part):
        to = (t + i) % NT
        rows = pl.ds(pl.multiple_of((to // 2) * PART + HALF * part, HALF), HALF)
        return remote(mids.at[rows], midr.at[part, t], sm.at[part, i], rm.at[part, i], {"tm": to})

    for part in range(2):
        for i in (5, 3, 1, 7, 4, 2, 6):
            mid_copy(i, part).start()
        midr[part, t] = mids[pl.ds(pl.multiple_of(y * PART + HALF * part, HALF), HALF), :]

    loc_q.wait()
    loc_o.wait()
    for unit, way in ((2, 0), (3, 0), (0, 1), (1, 1)):
        wq_send(unit, way).wait_recv()
    for unit, way in ((0, 0), (2, 1), (1, 0), (3, 1)):
        wq_pass(unit, way).wait_recv()

    tokens = NT * HALF
    same = (lax.broadcasted_iota(jnp.int32, (tokens, tokens), 0) % HALF) == (
        lax.broadcasted_iota(jnp.int32, (tokens, tokens), 1) % HALF
    )
    keep = jnp.where(xh == 0, 1.0, 0.0).astype(F32)
    ones = jnp.ones((8, tokens), F32)

    def fin_copy(f, part):
        return remote(
            fins.at[part, f], finr.at[t, pl.ds(HALF * part, HALF)], sf.at[part, f], rf.at[part, t],
            {"section": nxt, "tm": f},
        )

    for part in range(2):
        for i in range(1, NT):
            mid_copy(i, part).wait_recv()
        middle = midr[part].reshape(tokens, D).astype(F32)
        centred = middle - jnp.mean(middle, axis=-1, keepdims=True)
        variance = jnp.mean(centred * centred, axis=-1, keepdims=True)
        normed = (centred * lax.rsqrt(variance + 1e-06) * (1.0 + sc_ref[...]) + sh_ref[...]).astype(BF16)
        proj[...] = lax.dot_general(
            normed, wq[...].reshape(12 * 144, D), (((1,), (1,)), ((), ())), preferred_element_type=F32
        ).T
        for head in range(8):
            at = 432 * (head // 2) + HD * (head % 2)
            tq = proj[at : at + HD, :].astype(BF16)
            tk = proj[at + 144 : at + 144 + HD].T.astype(BF16)
            tv = jnp.concatenate([proj[at + 288 : at + 288 + HD], ones], axis=0).astype(BF16)
            s = jnp.where(same, jnp.dot(tk, tq, preferred_element_type=F32), -jnp.inf)
            p = jnp.exp2((s - jnp.max(s, axis=0, keepdims=True)) * FACTOR2).astype(BF16)
            o = jnp.dot(tv, p, preferred_element_type=F32)
            mixt[HD * head : HD * (head + 1), :] = o[:HD] / o[HD : HD + 1]
        mixed = mixt[...].T.astype(BF16)
        summed = jnp.dot(mixed, wo[...].reshape(576, D), preferred_element_type=F32)
        done = keep * middle + gt_ref[...] * summed
        fins[part] = done.astype(BF16).reshape(NT, HALF, D)
        for f in range(NT):
            fin_copy(f, part).start()

    def fin_wait(f, c):
        for part in range(2):
            remote(
                fins.at[part, f], finr.at[f, pl.ds(HALF * part, HALF)], sf.at[part, f], rf.at[part, f],
                {"section": nxt, "tm": f},
            ).wait_recv()
        return c

    lax.fori_loop(0, NT, fin_wait, 0)

    def left_z(i, c):
        kv_copy(i).wait_send()
        q_copy(i).wait_send()
        o_copy(i).wait_send()
        return c

    lax.fori_loop(1, NZ, left_z, 0)

    for k in range(1, 4):
        wz_far(k).wait_send()
    for i in range(4):
        wz_near(i).wait_send()
        wy_copy(i).wait_send() if i < 2 else wy_pass(i - 2).wait_send()
        wx_copy(i).wait_send()
        for way in range(2):
            wq_send(i, way).wait_send()
    for unit, way in ((0, 0), (2, 1), (1, 0), (3, 1)):
        wq_pass(unit, way).wait_send()

    def left_t(i, c):
        mid_copy(i, 0).wait_send()
        mid_copy(i, 1).wait_send()
        return c

    lax.fori_loop(1, NT, left_t, 0)

    def left_f(f, c):
        fin_copy(f, 0).wait_send()
        fin_copy(f, 1).wait_send()
        return c

    lax.fori_loop(0, NT, left_f, 0)


def shards(
    hidden_in, query_s, key_s, value_s, out_proj_s, gate_s, shift_t, scale_t, qkv_t, out_t, gate_t
):
    vm = pl.BlockSpec(memory_space=pltpu.VMEM)
    hbm = pl.BlockSpec(memory_space=pl.ANY)
    dma = pltpu.SemaphoreType.DMA
    plane = (HD, ROWS)
    out = pl.pallas_call(
        kernel,
        out_shape=jax.ShapeDtypeStruct((NT, PART, D), BF16),
        in_specs=[hbm, hbm, hbm, hbm, hbm, vm, vm, vm, hbm, hbm, vm],
        out_specs=hbm,
        scratch_shapes=[
            pltpu.VMEM((ROWS, D), BF16),
            pltpu.VMEM((ROWS, D), BF16),
            pltpu.VMEM((ROWS, D), BF16),
            pltpu.VMEM((HD, D), BF16),
            pltpu.VMEM((NZ, 2 * HD, ROWS), BF16),
            pltpu.VMEM((NZ, 2 * HD, ROWS), BF16),
            pltpu.VMEM((NZ, *plane), BF16),
            pltpu.VMEM((NZ, *plane), BF16),
            pltpu.VMEM((NZ, *plane), BF16),
            pltpu.VMEM((NZ, *plane), BF16),
            pltpu.VMEM((80, 128), BF16),
            pltpu.VMEM((NT, 4, 4, 88, 128), BF16),
            pltpu.VMEM((NZ, HD, D), BF16),
            pltpu.VMEM((ROWS, D), F32),
            pltpu.VMEM((NZ * ROWS, HD), BF16),
            pltpu.VMEM((HD + 8, NZ * ROWS), BF16),
            pltpu.VMEM((4, 3, 144, D), BF16),
            pltpu.VMEM((4, 144, D), BF16),
            pltpu.VMEM((ROWS, D), BF16),
            pltpu.VMEM((ROWS, D), BF16),
            pltpu.VMEM((2, NT, HALF, D), BF16),
            pltpu.VMEM((1728, NT * HALF), F32),
            pltpu.VMEM((576, NT * HALF), F32),
            pltpu.VMEM((2, NT, HALF, D), BF16),
            dma((NZ,)), dma((NZ,)), dma((NZ,)), dma((NZ,)), dma((NZ,)), dma((NZ,)),
            dma((8,)), dma((8,)), dma((4,)), dma((4,)), dma((4,)), dma((4,)),
            dma((2, 8)), dma((2, 8)), dma((2, NT)), dma((2, NT)), dma((2, NT)), dma((2, NT)), dma((7,)),
        ],
        compiler_params=pltpu.CompilerParams(
            collective_id=0, has_side_effects=True, vmem_limit_bytes=56 * 1024 * 1024
        ),
        cost_estimate=pl.CostEstimate(flops=3_000_000_000, bytes_accessed=6_000_000, transcendentals=4_500_000),
        name="st_block_pair",
    )(
        query_s[0, 0], key_s[0, 0], value_s[0, 0], hidden_in[0, 0], out_proj_s[0],
        gate_s, shift_t, scale_t, qkv_t[0], out_t[0], gate_t,
    )
    halves = out.reshape(4, 2, PART, D)
    return (halves[:, 0] + halves[:, 1]).reshape(1, 1, ROWS, D)


def solution(mesh):
    in_specs = (
        P("section", "tm", "space", None),
        P("section", "tm", "space", None),
        P("section", "tm", "space", None),
        P("section", "tm", "space", None),
        P("section", "space", None),
        P("section", None),
        P("section", None),
        P("section", None),
        P("section", None, "tm", None),
        P("section", "tm", None),
        P("section", None),
    )
    out_specs = P("section", "tm", "space", None)
    return jax.shard_map(shards, mesh=mesh, in_specs=in_specs, out_specs=out_specs, check_vma=False)
```

time: 117 us -> 108 us (0.923)
  Pallas kernels: 115 us -> 106 us
    pallas_call x1, Pallas kernels: 115 us -> 106 us  [shards(): pl.pallas_call(kernel, out_shape=jax.ShapeDtypeStruct((NT, PART, D), BF16...]
    convert_element_type x2 -> x0, other arithmetic: 1.92 us -> none  [the longest x1 1.15 us: shards(): halves = out.reshape(4, 2, PART, D).astype(F32)]
    add x0 -> x1, other arithmetic: none -> 1.81 us  [shards(): return (halves[:, 0] + halves[:, 1]).reshape(1, 1, ROWS, D)]
where the time goes in v3:
time: 108 us
  Pallas kernels  106 us (98%)
  other arithmetic  1.81 us (2%)
    pallas_call x1, Pallas kernels, shards(): pl.pallas_call(kernel, out_shape=jax.ShapeDtypeStruct((NT, PART, D), BF16...  106 us

profile of v3, /device:TPU:1, one launch (start us, length us, event | category | flops | bytes accessed | tf_op | source)
XLA Modules:
  0.0 107.8 jit_solution(11993395588858431833)
XLA Ops:
  0.0 106.0 %st_block_pair.1 = bf16[8,32,1152]{2,1,0:T(8,128)(2,1)} custom-call(bf16[128,1152]{1,0:T(8,128)(2,1)} %bitcast.12, bf16[128,1152]{1,0:T(8,128)(2,1)} %bitcast.13, bf16[128,1152]{1,0:T(8,128)(2,1)} %bitcast.14, bf16[128,1152]{1,0:T(8,128)(2,1)} %bitcast.15, bf16[72,1152]{1,0:T(8,128)(2,1)} %bitcast.16, f32[1,1152]{1,0:T(1,128)} %gs_ref.1, f32[1,1152]{1,0:T(1,128)} %sh_ref.1, ...), custom_call_target="tpu_custom_call" | custom-call | flops 3000000000 | bytes 6000000 | tf_op jit(solution)/shard_map/st_block_pair/pallas_call | solution.py:399
  106.0 1.8 %slice_add_fusion = bf16[4,1,32,1152]{3,2,1,0:T(8,128)(2,1)} fusion(bf16[4,2,32,1152]{3,2,1,0:T(8,128)(2,1)} %bitcast.9), kind=kLoop, calls=%fused_computation | loop fusion | flops 147456 | bytes 884736 | tf_op jit(solution)/shard_map/add | solution.py:443

commit v4 on v3

--- a/solution.py
+++ b/solution.py
@@ -16,7 +16,7 @@
 ROWS = 128
 PART = 32
 HALF = 16
-PACE = (2, 1)
+PACE = (2, 1, 1, 1)
 KV1 = 5
 FACTOR = HD ** (-0.5)
 FACTOR2 = FACTOR * 1.4426950408889634
@@ -57,20 +57,8 @@
         pl.semaphore_signal(barrier, inc=1, device_id={"space": (z + i) % NZ}, device_id_type=MESH)
         return c
 
-    lax.fori_loop(1, NZ, greet_z, 0)
-
-    def greet_t(i, c):
-        pl.semaphore_signal(barrier, inc=1, device_id={"tm": (t + i) % NT}, device_id_type=MESH)
-        return c
-
-    lax.fori_loop(1, NT, greet_t, 0)
-
-    def greet_s(i, c):
-        pl.semaphore_signal(barrier, inc=1, device_id={"section": nxt, "tm": i}, device_id_type=MESH)
-        pl.semaphore_signal(barrier, inc=1, device_id={"section": prv, "tm": i}, device_id_type=MESH)
-        return c
-
-    lax.fori_loop(0, NT, greet_s, 0)
+    greet_z(8, 0)
+    lax.fori_loop(1, 8, lambda i, c: greet_z(8 + i, greet_z(8 - i, c)), 0)
 
     loc_in = [
         pltpu.make_async_copy(a, b, loc.at[3 + i])
@@ -78,6 +66,19 @@
     ]
     for c in loc_in:
         c.start()
+    def greet_t(i, c):
+        pl.semaphore_signal(barrier, inc=1, device_id={"tm": (t + i) % NT}, device_id_type=MESH)
+        return c
+
+    lax.fori_loop(1, NT, greet_t, 0)
+
+    def greet_s(i, c):
+        pl.semaphore_signal(barrier, inc=1, device_id={"section": nxt, "tm": i}, device_id_type=MESH)
+        pl.semaphore_signal(barrier, inc=1, device_id={"section": prv, "tm": i}, device_id_type=MESH)
+        return c
+
+    lax.fori_loop(0, NT, greet_s, 0)
+
     loc_q = pltpu.make_async_copy(qkv_hbm, wq.at[y], loc.at[0])
     loc_o = pltpu.make_async_copy(ot_hbm, wo.at[y], loc.at[1])
     loc_h = pltpu.make_async_copy(hid_hbm, hid, loc.at[2])
@@ -105,16 +106,19 @@
     def wz_far(k):
         return remote(ws.at[t, 0, 0], ws.at[t, 0, 4 - k], swz.at[k], rwz.at[k], {"space": (z + 4 * k) % NZ})
 
+    def wz_opposite():
+        return remote(ws.at[t, 0, 3], ws.at[t, 0, 2], swz.at[2], rwz.at[2], {"space": (z + 4) % NZ})
+
     def wz_near(i):
-        to, src, dst = (
-            ((z + NZ - 1) % NZ, ws.at[t, 0], ws.at[t, 1]),
-            ((z + 1) % NZ, ws.at[t, 0], ws.at[t, 3]),
-            ((z + NZ - 2) % NZ, ws.at[t, 0, pl.ds(2, 2)], ws.at[t, 2, pl.ds(2, 2)]),
-            ((z + 2) % NZ, ws.at[t, 0, pl.ds(1, 2)], ws.at[t, 2, pl.ds(0, 2)]),
+        dev, src, dst = (
+            (zl, ws.at[t, 0], ws.at[t, 1]),
+            (zr, ws.at[t, 0], ws.at[t, 3]),
+            (zl, ws.at[t, 1, pl.ds(2, 2)], ws.at[t, 2, pl.ds(2, 2)]),
+            (zr, ws.at[t, 3, pl.ds(1, 2)], ws.at[t, 2, pl.ds(0, 2)]),
         )[i]
-        return remote(src, dst, swz.at[4 + i], rwz.at[4 + i], {"space": to})
-
-    for k in (2, 1, 3):
+        return remote(src, dst, swz.at[4 + i], rwz.at[4 + i], dev)
+
+    for k in (1, 3):
         wz_far(k).start()
 
     def wq_send(unit, way):
@@ -181,13 +185,21 @@
     issue(PACE[0])
     vmat[HD:, :] = jnp.ones((8, NZ * ROWS), BF16)
     take_kv(z)
-    for k in (1, 3, 2):
-        wz_far(k).wait_recv()
-    for i in range(4):
-        wz_near(i).start()
+    wz_far(1).wait_recv()
+    wz_opposite().start()
+    wz_far(3).wait_recv()
     issue(PACE[1])
-    for i in range(4):
-        wz_near(i).wait_recv()
+    wz_opposite().wait_recv()
+    wz_near(0).start()
+    wz_near(1).start()
+    issue(PACE[2])
+    wz_near(0).wait_recv()
+    wz_near(2).start()
+    wz_near(1).wait_recv()
+    wz_near(3).start()
+    issue(PACE[3])
+    wz_near(2).wait_recv()
+    wz_near(3).wait_recv()
     wx_copy(0).start()
     wy_copy(0).start()
     wy_copy(1).start()
@@ -363,8 +375,9 @@
 
     lax.fori_loop(1, NZ, left_z, 0)
 
-    for k in range(1, 4):
-        wz_far(k).wait_send()
+    wz_far(1).wait_send()
+    wz_far(3).wait_send()
+    wz_opposite().wait_send()
     for i in range(4):
         wz_near(i).wait_send()
         wy_copy(i).wait_send() if i < 2 else wy_pass(i - 2).wait_send()

time: 108 us -> 106 us (0.981)
  Pallas kernels: 106 us -> 104 us
    pallas_call x1, Pallas kernels: 106 us -> 104 us  [shards(): pl.pallas_call(kernel, out_shape=jax.ShapeDtypeStruct((NT, PART, D), BF16...]
where the time goes in v4:
time: 106 us
  Pallas kernels  104 us (98%)
  other arithmetic  1.81 us (2%)
    pallas_call x1, Pallas kernels, shards(): pl.pallas_call(kernel, out_shape=jax.ShapeDtypeStruct((NT, PART, D), BF16...  104 us

profile of v4, /device:TPU:1, one launch (start us, length us, event | category | flops | bytes accessed | tf_op | source)
XLA Modules:
  0.0 106.0 jit_solution(11065771042468990669)
XLA Ops:
  0.0 104.2 %st_block_pair.1 = bf16[8,32,1152]{2,1,0:T(8,128)(2,1)} custom-call(bf16[128,1152]{1,0:T(8,128)(2,1)} %bitcast.12, bf16[128,1152]{1,0:T(8,128)(2,1)} %bitcast.13, bf16[128,1152]{1,0:T(8,128)(2,1)} %bitcast.14, bf16[128,1152]{1,0:T(8,128)(2,1)} %bitcast.15, bf16[72,1152]{1,0:T(8,128)(2,1)} %bitcast.16, f32[1,1152]{1,0:T(1,128)} %gs_ref.1, f32[1,1152]{1,0:T(1,128)} %sh_ref.1, ...), custom_call_target="tpu_custom_call" | custom-call | flops 3000000000 | bytes 6000000 | tf_op jit(solution)/shard_map/st_block_pair/pallas_call | solution.py:412
  104.2 1.8 %slice_add_fusion = bf16[4,1,32,1152]{3,2,1,0:T(8,128)(2,1)} fusion(bf16[4,2,32,1152]{3,2,1,0:T(8,128)(2,1)} %bitcast.9), kind=kLoop, calls=%fused_computation | loop fusion | flops 147456 | bytes 884736 | tf_op jit(solution)/shard_map/add | solution.py:456

commit v5 on v4

--- a/solution.py
+++ b/solution.py
@@ -95,11 +95,7 @@
     vt = v_ref[...].astype(F32).T
     for h in range(NZ):
         kvs[h] = jnp.concatenate([kt[HD * h : HD * (h + 1)], vt[HD * h : HD * (h + 1)]], axis=0).astype(BF16)
-    qt = q_ref[...].astype(F32).T
-    for h in range(NZ):
-        qs[h] = qt[HD * h : HD * (h + 1)].astype(BF16)
     kvr[z] = kvs[z]
-    qr[z] = qs[z]
 
     pl.semaphore_wait(barrier, (NZ - 1) + (NT - 1) + 2 * NT)
 
@@ -183,6 +179,10 @@
             start(what)
 
     issue(PACE[0])
+    qt = q_ref[...].astype(F32).T
+    for h in range(NZ):
+        qs[h] = qt[HD * h : HD * (h + 1)].astype(BF16)
+    qr[z] = qs[z]
     vmat[HD:, :] = jnp.ones((8, NZ * ROWS), BF16)
     take_kv(z)
     wz_far(1).wait_recv()
@@ -256,7 +256,7 @@
             wy_pass(1).wait_recv()
             wx_copy(3).start()
 
-        @pl.when(i == 4)
+        @pl.when(i == 2)
         def _():
             for unit, way in ((0, 0), (2, 1), (1, 0), (3, 1)):
                 wq_send(unit, way).wait_recv()

time: 106 us -> 106 us (level)
  no operation moved by 1% of the time
where the time goes in v5:
time: 106 us
  Pallas kernels  104 us (98%)
  other arithmetic  1.81 us (2%)
    pallas_call x1, Pallas kernels, shards(): pl.pallas_call(kernel, out_shape=jax.ShapeDtypeStruct((NT, PART, D), BF16...  104 us

profile of v5, /device:TPU:1, one launch (start us, length us, event | category | flops | bytes accessed | tf_op | source)
XLA Modules:
  0.0 106.0 jit_solution(12322576149524054296)
XLA Ops:
  0.0 104.2 %st_block_pair.1 = bf16[8,32,1152]{2,1,0:T(8,128)(2,1)} custom-call(bf16[128,1152]{1,0:T(8,128)(2,1)} %bitcast.12, bf16[128,1152]{1,0:T(8,128)(2,1)} %bitcast.13, bf16[128,1152]{1,0:T(8,128)(2,1)} %bitcast.14, bf16[128,1152]{1,0:T(8,128)(2,1)} %bitcast.15, bf16[72,1152]{1,0:T(8,128)(2,1)} %bitcast.16, f32[1,1152]{1,0:T(1,128)} %gs_ref.1, f32[1,1152]{1,0:T(1,128)} %sh_ref.1, ...), custom_call_target="tpu_custom_call" | custom-call | flops 3000000000 | bytes 6000000 | tf_op jit(solution)/shard_map/st_block_pair/pallas_call | solution.py:412
  104.2 1.8 %slice_add_fusion = bf16[4,1,32,1152]{3,2,1,0:T(8,128)(2,1)} fusion(bf16[4,2,32,1152]{3,2,1,0:T(8,128)(2,1)} %bitcast.9), kind=kLoop, calls=%fused_computation | loop fusion | flops 147456 | bytes 884736 | tf_op jit(solution)/shard_map/add | solution.py:456
